TPU v7x, 32 devices: a whole 2x2x4 slice. The times are simulated.
32 devices in a mesh: node: 8 (over y, x, core), dev: 4 (over z).
Axes of the slice: x: 2, y: 2, z: 4, core: 2. Of those that a mesh axis runs over, the one named last changes fastest.
Arguments:
- tokens: bfloat16 [128, 4096], P('node', 'dev'), may hold values from -6 to 6
- routes: int32 [128, 8], P('node'), may hold values from 0 to 7, as said below
- gate_codes: int32 [128, 8], P('node'), may hold values from 1 to 65535
- w_gate: bfloat16 [8, 4096, 2048], P('node', None, 'dev'), may hold values from -0.09375 to 0.09375
- w_up: bfloat16 [8, 4096, 2048], P('node', None, 'dev'), may hold values from -0.09375 to 0.09375
- w_down: bfloat16 [8, 2048, 4096], P('node', 'dev'), may hold values from -0.125 to 0.125
- cotangent: bfloat16 [128, 4096], P('node', 'dev'), may hold values from -6 to 6
Outputs:
- layer_out: bfloat16 [128, 4096], P('node', 'dev')
- token_grad: bfloat16 [128, 4096], P('node', 'dev')
- down_grad: bfloat16 [8, 2048, 4096], P('node', 'dev')
Inputs may be any that keep to these rules, and one draw needn't show every extreme that they name: `routes`: each token names 8 different experts, taken from at most 4 groups of 4 consecutive experts. Among the 16 tokens of one block (one index of node), no expert is named by more than 16 tokens, and in every block some expert is named by exactly 16.
All inputs are finite; a program needn't handle non-finite values.
Results may differ from a plain program's by a relative error of at most 0.012.
Values may be sent and summed in bfloat16 or wider, within the bound.
A program may use at most 64 MiB of HBM per device.

v0:
```python
import jax
import jax.numpy as jnp
from jax import lax
from jax.sharding import PartitionSpec as P

TOP_GROUPS = 4
GROUP_SIZE = 4
exact_mode = lax.Precision.HIGHEST


def slot_layout(routes, gate_codes, experts, capacity):
    tokens_here = routes.shape[0]
    member = (routes[:, :, None] == jnp.arange(experts, dtype=jnp.int32)[None, None, :]).astype(
        jnp.float32
    )
    named_by = jnp.sum(member, axis=1)
    earlier = (jnp.arange(tokens_here)[:, None] > jnp.arange(tokens_here)[None, :]).astype(
        jnp.float32
    )
    before = jnp.dot(earlier, named_by, precision=exact_mode)
    placed = named_by[:, :, None] * (
        before[:, :, None] == jnp.arange(capacity).astype(jnp.float32)[None, None, :]
    ).astype(jnp.float32)
    weights = gate_codes.astype(jnp.float32) / 65536.0
    gating = jnp.sum(member * weights[:, :, None], axis=1)
    return (placed, gating)


def deliver(local_rows, build, fold, initial):
    whole_rows = lax.all_gather(local_rows, "dev", axis=1, tiled=True)
    arrived = lax.all_to_all(build(whole_rows), "node", split_axis=0, concat_axis=0, tiled=True)
    return fold(initial, arrived, 0)


def send_back(partial_value):
    shares = lax.psum_scatter(
        partial_value.astype(jnp.bfloat16), "dev", scatter_dimension=2, tiled=True
    )
    return lax.all_to_all(shares, "node", split_axis=0, concat_axis=0, tiled=True)


def on_device(tokens, routes, gate_codes, w_gate, w_up, w_down, cotangent):
    experts = lax.axis_size("node")
    groups = experts // GROUP_SIZE
    chosen_count = min(TOP_GROUPS, groups)
    capacity = tokens.shape[0] * chosen_count // groups
    placed, gating = slot_layout(routes, gate_codes, experts, capacity)
    place_low = placed.astype(jnp.bfloat16)
    weighted = placed * gating[:, :, None]
    gate_mat = w_gate[0]
    up_mat = w_up[0]
    down_mat = w_down[0]
    hidden_width = gate_mat.shape[1]

    def spread_tokens(payload):
        return jnp.einsum(
            "tep,tf->epf", place_low, payload, preferred_element_type=jnp.float32
        ).astype(jnp.bfloat16)

    def spread_cotangent(payload):
        return jnp.einsum(
            "tep,tf->epf", weighted, payload.astype(jnp.float32), precision=exact_mode
        ).astype(jnp.bfloat16)

    def project_in(totals, portion, offset):
        gate_next = jnp.einsum("epf,fh->eph", portion, gate_mat, preferred_element_type=jnp.float32)
        up_next = jnp.einsum("epf,fh->eph", portion, up_mat, preferred_element_type=jnp.float32)
        return (gate_next, up_next)

    empty_hidden = jnp.zeros((experts, capacity, hidden_width), jnp.float32)
    gate_pre, up_pre = deliver(tokens, spread_tokens, project_in, (empty_hidden, empty_hidden))
    squash = jax.nn.sigmoid(gate_pre)
    hidden = (gate_pre * squash * up_pre).astype(jnp.bfloat16)
    partial_value = jnp.einsum("eph,hf->epf", hidden, down_mat, preferred_element_type=jnp.float32)
    returned = send_back(partial_value)
    layer_out = jnp.einsum(
        "tep,epf->tf", weighted, returned.astype(jnp.float32), precision=exact_mode
    ).astype(jnp.bfloat16)

    def project_cotangent(totals, portion, offset):
        grad_next = jnp.einsum("epf,hf->eph", portion, down_mat, preferred_element_type=jnp.float32)
        block_grad = jnp.einsum("eph,epf->hf", hidden, portion, preferred_element_type=jnp.float32)
        return (grad_next, block_grad)

    empty_down = jnp.zeros((hidden_width, down_mat.shape[1]), jnp.float32)
    hidden_grad, down_total = deliver(
        cotangent, spread_cotangent, project_cotangent, (empty_hidden, empty_down)
    )
    gate_grad = (hidden_grad * up_pre * squash * (1.0 + gate_pre * (1.0 - squash))).astype(
        jnp.bfloat16
    )
    up_grad = (hidden_grad * gate_pre * squash).astype(jnp.bfloat16)
    partial_back = jnp.einsum(
        "eph,fh->epf", gate_grad, gate_mat, preferred_element_type=jnp.float32
    )
    partial_back = partial_back + jnp.einsum(
        "eph,fh->epf", up_grad, up_mat, preferred_element_type=jnp.float32
    )
    returned_back = send_back(partial_back)
    token_grad = jnp.einsum(
        "tep,epf->tf", placed, returned_back.astype(jnp.float32), precision=exact_mode
    ).astype(jnp.bfloat16)
    return (layer_out, token_grad, down_total.astype(jnp.bfloat16)[None])


def solution(mesh):
    in_specs = (
        P("node", "dev"),
        P("node", None),
        P("node", None),
        P("node", None, "dev"),
        P("node", None, "dev"),
        P("node", "dev", None),
        P("node", "dev"),
    )
    out_specs = (P("node", "dev"), P("node", "dev"), P("node", "dev", None))
    return jax.shard_map(
        on_device, mesh=mesh, in_specs=in_specs, out_specs=out_specs, check_vma=False
    )
```

profile of v0, /device:TPU:0, one launch (start us, length us, event | category | flops | bytes accessed | tf_op | source)
XLA Modules:
  0.0 132.5 jit_solution(16287439819941731388)
XLA Ops:
  7.2 0.7 convert_multiply_fusion
  7.9 0.7 select_reduce_fusion
  8.6 0.1 fusion.38
  8.7 15.3 %all_gather.6 = bf16[16,4096]{1,0:T(8,128)(2,1)S(1)} all-gather(bf16[16,1024]{1,0:T(8,128)(2,1)} %param.7), channel_id=1, replica_groups=mesh['node'=8,'dev'=4] {'dev'}, dimensions={1}, use_global_device_ids=true | all-gather | bytes 163840 | tf_op jit(solution)/shard_map/all_gather | solution.py:30
  24.0 1.5 %convolution_convert_fusion.2 = bf16[8,16,4096]{2,1,0:T(8,128)(2,1)} fusion(bf16[16,4096]{1,0:T(8,128)(2,1)S(1)} %all_gather.6, f32[16,8]{0,1:T(8,128)S(1)} %get-tuple-element.4, f32[16]{0:T(128)S(1)} %iota_convert_fusion, f32[16,8]{0,1:T(8,128)S(1)} %fusion.38), kind=kOutput, calls=%fused_computation.6 | convolution fusion | flops 17305600 | bytes 1180736 | tf_op jit(solution)/shard_map/tep,tf->epf/dot_general | solution.py:56
  25.5 3.7 %all-to-all-start = ((bf16[8,16,4096]{2,1,0:T(8,128)(2,1)}), bf16[8,16,4096]{2,1,0:T(8,128)(2,1)S(1)}, u32[]{:S(2)}, u32[]{:S(2)}) async-start(bf16[8,16,4096]{2,1,0:T(8,128)(2,1)} %convolution_convert_fusion.2), calls=%async_computation | async-start | bytes 2097152 | tf_op jit(solution)/shard_map/all_to_all | solution.py:31
  29.2 13.7 %all_gather.7 = bf16[16,4096]{1,0:T(8,128)(2,1)S(1)} all-gather(bf16[16,1024]{1,0:T(8,128)(2,1)} %param.13), channel_id=1, replica_groups=mesh['node'=8,'dev'=4] {'dev'}, dimensions={1}, use_global_device_ids=true | all-gather | bytes 163840 | tf_op jit(solution)/shard_map/all_gather | solution.py:30
  42.8 2.1 %convolution_convert_fusion = bf16[8,16,4096]{2,1,0:T(8,128)(2,1)} fusion(bf16[16,4096]{1,0:T(8,128)(2,1)S(1)} %all_gather.7, f32[16,8]{0,1:T(8,128)S(1)} %get-tuple-element.3, f32[16,8]{0,1:T(8,128)S(1)} %get-tuple-element.4, f32[16]{0:T(128)S(1)} %iota_convert_fusion, f32[16,8]{0,1:T(8,128)S(1)} %fusion.38), kind=kOutput, calls=%fused_computation.4 | convolution fusion | flops 101193728 | bytes 1181248 | tf_op jit(solution)/shard_map/tep,tf->epf/dot_general | solution.py:61
  44.9 4.1 %all-to-all-start.2 = ((bf16[8,16,4096]{2,1,0:T(8,128)(2,1)}), bf16[8,16,4096]{2,1,0:T(8,128)(2,1)S(1)}, u32[]{:S(2)}, u32[]{:S(2)}) async-start(bf16[8,16,4096]{2,1,0:T(8,128)(2,1)} %convolution_convert_fusion), calls=%async_computation.3 | async-start | bytes 2097152 | tf_op jit(solution)/shard_map/all_to_all | solution.py:31
  49.0 0.0 reduce-scatter.3.cloned.1.call-start
  49.1 0.0 copy-start.2
  49.1 3.1 %fusion.10 = f32[8,16,512]{2,1,0:T(8,128)S(1)} fusion(bf16[8,16,4096]{2,1,0:T(8,128)(2,1)S(1)} %all-to-all-done, bf16[1,4096,512]{2,1,0:T(8,128)(2,1)} %param.10), kind=kOutput, calls=%fused_computation.15 | convolution fusion | flops 536870912 | bytes 5505024 | tf_op jit(solution)/shard_map/epf,fh->eph/dot_general | solution.py:66
  52.1 0.4 copy-done.2
  52.5 0.8 multiply_convert_fusion.2
  53.3 1.4 %copy-done = bf16[1,512,4096]{2,1,0:T(8,128)(2,1)S(1)} copy-done((bf16[1,512,4096]{2,1,0:T(8,128)(2,1)S(1)}, bf16[1,512,4096]{2,1,0:T(8,128)(2,1)}, u32[]{:S(2)}) %copy-start) | copy-done | bytes 4194328
  54.7 1.7 %convolution_convert_fusion.1 = bf16[8,16,4096]{2,1,0:T(8,128)(2,1)} fusion(bf16[8,16,512]{2,1,0:T(8,128)(2,1)S(1)} %get-tuple-element.5, bf16[1,512,4096]{2,1,0:T(8,128)(2,1)S(1)} %copy-done), kind=kOutput, calls=%fused_computation.5 | convolution fusion | flops 537395200 | bytes 5373952 | tf_op jit(solution)/shard_map/eph,hf->epf/dot_general | solution.py:74
  56.4 0.0 reduce-scatter.3.cloned.1.call-update
  56.5 0.0 reduce-scatter.5.cloned.1.call-start
  56.5 7.9 %all-to-all-done.2 = bf16[8,16,4096]{2,1,0:T(8,128)(2,1)S(1)} async-done(((bf16[8,16,4096]{2,1,0:T(8,128)(2,1)}), bf16[8,16,4096]{2,1,0:T(8,128)(2,1)S(1)}, u32[]{:S(2)}, u32[]{:S(2)}) %all-to-all-start.2) | async-done | bytes 1048608 | tf_op jit(solution)/shard_map/all_to_all | solution.py:31
  64.4 3.9 %fusion.2 = f32[8,16,512]{2,1,0:T(8,128)S(1)} fusion(bf16[8,16,4096]{2,1,0:T(8,128)(2,1)S(1)} %all-to-all-done.2, bf16[1,512,4096]{2,1,0:T(8,128)(2,1)} %param.12), kind=kOutput, calls=%fused_computation.7 | convolution fusion | flops 536870912 | bytes 5505024 | tf_op jit(solution)/shard_map/epf,hf->eph/dot_general | solution.py:81
  68.3 1.5 %fusion.8 = f32[8,16,4096]{2,1,0:T(8,128)S(1)} fusion(bf16[1,4096,512]{2,1,0:T(8,128)(2,1)S(1)} %copy-done.1, f32[8,16,512]{2,1,0:T(8,128)S(1)} %fusion.10, f32[8,16,512]{2,1,0:T(8,128)S(1)} %fusion.2, f32[8,16,512]{2,1,0:T(8,128)S(1)} %get-tuple-element.6), kind=kOutput, calls=%fused_computation.13 | convolution fusion | flops 537526272 | bytes 7077888 | tf_op jit(solution)/shard_map/eph,fh->epf/dot_general | solution.py:93
  69.8 0.7 copy-done.3
  70.5 2.5 %fusion.1 = bf16[8,16,4096]{2,1,0:T(8,128)(2,1)} fusion(f32[8,16,4096]{2,1,0:T(8,128)S(1)} %fusion.8, bf16[1,4096,512]{2,1,0:T(8,128)(2,1)S(1)} %copy-done.3, f32[8,16,512]{2,1,0:T(8,128)S(1)} %fusion.2, f32[8,16,512]{2,1,0:T(8,128)S(1)} %fusion.10), kind=kOutput, calls=%fused_computation.3 | convolution fusion | flops 538312704 | bytes 7864320 | tf_op jit(solution)/shard_map/eph,fh->epf/dot_general | solution.py:96
  73.0 0.0 reduce-scatter.5.cloned.1.call-update
  73.0 12.7 %reduce-scatter.3.cloned.1.call-done = bf16[8,16,1024]{2,1,0:T(8,128)(2,1)} async-done(((bf16[8,16,4096]{2,1,0:T(8,128)(2,1)}), bf16[8,16,1024]{2,1,0:T(8,128)(2,1)}) %reduce-scatter.3.cloned.1.call-update) | async-done | bytes 262160 | tf_op jit(solution)/shard_map/reduce_scatter | solution.py:36
  85.7 3.6 %all-to-all-start.1 = ((bf16[8,16,1024]{2,1,0:T(8,128)(2,1)}), bf16[8,16,1024]{2,1,0:T(8,128)(2,1)S(1)}, u32[]{:S(2)}, u32[]{:S(2)}) async-start(bf16[8,16,1024]{2,1,0:T(8,128)(2,1)} %reduce-scatter.3.cloned.1.call-done), calls=%async_computation.2 | async-start | bytes 524288 | tf_op jit(solution)/shard_map/all_to_all | solution.py:39
  89.3 3.3 %fusion = bf16[1,512,4096]{2,1,0:T(8,128)(2,1)} fusion(bf16[8,16,512]{2,1,0:T(8,128)(2,1)S(1)} %get-tuple-element.5, bf16[8,16,4096]{2,1,0:T(8,128)(2,1)S(1)} %all-to-all-done.2), kind=kOutput, calls=%fused_computation.1 | convolution fusion | flops 538968064 | bytes 5373952 | tf_op jit(solution)/shard_map/eph,epf->hf/dot_general | solution.py:82
  92.6 21.3 %reduce-scatter.5.cloned.1.call-done = bf16[8,16,1024]{2,1,0:T(8,128)(2,1)} async-done(((bf16[8,16,4096]{2,1,0:T(8,128)(2,1)}), bf16[8,16,1024]{2,1,0:T(8,128)(2,1)}) %reduce-scatter.5.cloned.1.call-update) | async-done | bytes 262160 | tf_op jit(solution)/shard_map/reduce_scatter | solution.py:36
  113.9 3.6 %all-to-all-start.3 = ((bf16[8,16,1024]{2,1,0:T(8,128)(2,1)}), bf16[8,16,1024]{2,1,0:T(8,128)(2,1)S(1)}, u32[]{:S(2)}, u32[]{:S(2)}) async-start(bf16[8,16,1024]{2,1,0:T(8,128)(2,1)} %reduce-scatter.5.cloned.1.call-done), calls=%async_computation.5 | async-start | bytes 524288 | tf_op jit(solution)/shard_map/all_to_all | solution.py:39
  117.6 1.1 fusion.12
  118.7 5.8 %all-to-all-done.3 = bf16[8,16,1024]{2,1,0:T(8,128)(2,1)S(1)} async-done(((bf16[8,16,1024]{2,1,0:T(8,128)(2,1)}), bf16[8,16,1024]{2,1,0:T(8,128)(2,1)S(1)}, u32[]{:S(2)}, u32[]{:S(2)}) %all-to-all-start.3) | async-done | bytes 262176 | tf_op jit(solution)/shard_map/all_to_all | solution.py:39
  124.5 1.1 fusion.13
  (7 shorter events, 0.0 us)
Async XLA Ops:
  25.5 19.5 %all-to-all-start = ((bf16[8,16,4096]{2,1,0:T(8,128)(2,1)}), bf16[8,16,4096]{2,1,0:T(8,128)(2,1)S(1)}, u32[]{:S(2)}, u32[]{:S(2)}) async-start(bf16[8,16,4096]{2,1,0:T(8,128)(2,1)} %convolution_convert_fusion.2), calls=%async_computation | async-start | bytes 2097152 | tf_op jit(solution)/shard_map/all_to_all | solution.py:31
  44.9 19.5 %all-to-all-start.2 = ((bf16[8,16,4096]{2,1,0:T(8,128)(2,1)}), bf16[8,16,4096]{2,1,0:T(8,128)(2,1)S(1)}, u32[]{:S(2)}, u32[]{:S(2)}) async-start(bf16[8,16,4096]{2,1,0:T(8,128)(2,1)} %convolution_convert_fusion), calls=%async_computation.3 | async-start | bytes 2097152 | tf_op jit(solution)/shard_map/all_to_all | solution.py:31
  49.0 36.7 %reduce-scatter.3.cloned.1.call-start = ((), (), s32[]{:S(2)}) async-start(), calls=%async_computation.6 | async-start | bytes 1310720 | tf_op jit(solution)/shard_map/reduce_scatter | solution.py:36
  49.1 3.5 %copy-start.2 = (bf16[1,4096,512]{2,1,0:T(8,128)(2,1)S(1)}, bf16[1,4096,512]{2,1,0:T(8,128)(2,1)}, u32[]{:S(2)}) copy-start(bf16[1,4096,512]{2,1,0:T(8,128)(2,1)} %param.11) | copy-start | bytes 12582916
  52.5 2.2 %copy-start = (bf16[1,512,4096]{2,1,0:T(8,128)(2,1)S(1)}, bf16[1,512,4096]{2,1,0:T(8,128)(2,1)}, u32[]{:S(2)}) copy-start(bf16[1,512,4096]{2,1,0:T(8,128)(2,1)} %param.12) | copy-start | bytes 12582916
  56.5 57.5 %reduce-scatter.5.cloned.1.call-start = ((), (), s32[]{:S(2)}) async-start(), calls=%async_computation.7 | async-start | bytes 1310720 | tf_op jit(solution)/shard_map/reduce_scatter | solution.py:36
  64.4 3.9 %copy-start.1 = (bf16[1,4096,512]{2,1,0:T(8,128)(2,1)S(1)}, bf16[1,4096,512]{2,1,0:T(8,128)(2,1)}, u32[]{:S(2)}) copy-start(bf16[1,4096,512]{2,1,0:T(8,128)(2,1)} %param.10) | copy-start | bytes 12582916
  68.3 2.2 %copy-start.3 = (bf16[1,4096,512]{2,1,0:T(8,128)(2,1)S(1)}, bf16[1,4096,512]{2,1,0:T(8,128)(2,1)}, u32[]{:S(2)}) copy-start(bf16[1,4096,512]{2,1,0:T(8,128)(2,1)} %param.11) | copy-start | bytes 12582916
  85.7 28.2 %all-to-all-start.1 = ((bf16[8,16,1024]{2,1,0:T(8,128)(2,1)}), bf16[8,16,1024]{2,1,0:T(8,128)(2,1)S(1)}, u32[]{:S(2)}, u32[]{:S(2)}) async-start(bf16[8,16,1024]{2,1,0:T(8,128)(2,1)} %reduce-scatter.3.cloned.1.call-done), calls=%async_computation.2 | async-start | bytes 524288 | tf_op jit(solution)/shard_map/all_to_all | solution.py:39
  113.9 10.6 %all-to-all-start.3 = ((bf16[8,16,1024]{2,1,0:T(8,128)(2,1)}), bf16[8,16,1024]{2,1,0:T(8,128)(2,1)S(1)}, u32[]{:S(2)}, u32[]{:S(2)}) async-start(bf16[8,16,1024]{2,1,0:T(8,128)(2,1)} %reduce-scatter.5.cloned.1.call-done), calls=%async_computation.5 | async-start | bytes 524288 | tf_op jit(solution)/shard_map/all_to_all | solution.py:39
Sparse Core Ops, SparseCore 0:
  56.6 29.0 reduce-scatter.2
  88.1 25.7 reduce-scatter.4
where the time goes:
time: 133 us; the launch traced here: 132 us
  waiting for transfers between devices  47.7 us (36%)
  blocking collectives  28.9 us (22%)
  matrix products  22.7 us (17%)
  starting transfers between devices  15.2 us (11%)
  between operations  14.1 us (11%)
  local copies, waits for them, and re-layouts  2.48 us (2%)
  other arithmetic  1.4 us (1%)
    reduce_scatter x2, waiting for transfers between devices, send_back(): lax.psum_scatter(partial_value.astype(jnp.bfloat16), 'dev', scatter_dimen...  34 us
    all_gather x2, blocking collectives, deliver(): whole_rows = lax.all_gather(local_rows, 'dev', axis=1, tiled=True)  28.9 us
    all_to_all x2, waiting for transfers between devices, deliver(): lax.all_to_all(build(whole_rows), 'node', split_axis=0, concat_axis=0, ti...  7.91 us
    all_to_all x2, starting transfers between devices, deliver(): lax.all_to_all(build(whole_rows), 'node', split_axis=0, concat_axis=0, ti...  7.81 us
    all_to_all x2, starting transfers between devices, send_back(): lax.all_to_all(shares, 'node', split_axis=0, concat_axis=0, tiled=True)  7.29 us
    all_to_all x2, waiting for transfers between devices, send_back(): lax.all_to_all(shares, 'node', split_axis=0, concat_axis=0, tiled=True)  5.79 us
    dot_general x1, matrix products, project_cotangent(): jnp.einsum('epf,hf->eph', portion, down_mat, preferred_element_type=jnp.f...  3.88 us
    dot_general x1, matrix products, project_cotangent(): jnp.einsum('eph,epf->hf', hidden, portion, preferred_element_type=jnp.flo...  3.29 us
  transfers between devices with their start and end apart: 6, of which 4 were waited for; matrix products, arithmetic and copies ran while one was open for 15% of the time, Pallas kernels for 0%

commit v1 on v0

--- a/solution.py
+++ b/solution.py
@@ -28,7 +28,20 @@
 
 def deliver(local_rows, build, fold, initial):
     whole_rows = lax.all_gather(local_rows, "dev", axis=1, tiled=True)
-    arrived = lax.all_to_all(build(whole_rows), "node", split_axis=0, concat_axis=0, tiled=True)
+    x = build(whole_rows)
+    ways, here = (lax.axis_size("node"), lax.axis_index("node"))
+    width = x.shape[0] // ways
+    lengths = list(x.shape)
+    lengths[0] = width
+    height = lengths[0]
+    lengths[0] = height * ways
+    full = jnp.zeros(lengths, x.dtype)
+    for mask in range(ways):
+        part = lax.dynamic_slice_in_dim(x, (here ^ mask) * width, width, axis=0)
+        if mask:
+            part = lax.ppermute(part, "node", [(d, d ^ mask) for d in range(ways)])
+        full = lax.dynamic_update_slice_in_dim(full, part, (here ^ mask) * height, axis=0)
+    arrived = full
     return fold(initial, arrived, 0)
 
 

time: 133 us -> 140 us (1.053)
  waiting for transfers between devices: 47.7 us -> 54.7 us
  matrix products: 22.7 us -> 18.4 us
  starting transfers between devices: 15.2 us -> 18.8 us
    ppermute x0 -> x14, waiting for transfers between devices: none -> 20.1 us  [deliver(): part = lax.ppermute(part, 'node', [(d, d ^ mask) for d in range(ways)])]
    ppermute x0 -> x14, starting transfers between devices: none -> 11.4 us  [deliver(): part = lax.ppermute(part, 'node', [(d, d ^ mask) for d in range(ways)])]
    all_to_all x2 -> x0, waiting for transfers between devices: 7.91 us -> none  [deliver(): lax.all_to_all(build(whole_rows), 'node', split_axis=0, concat_axis=0, ti...]
    all_to_all x2 -> x0, starting transfers between devices: 7.81 us -> none  [deliver(): lax.all_to_all(build(whole_rows), 'node', split_axis=0, concat_axis=0, ti...]
    reduce_scatter x2, waiting for transfers between devices: 34 us -> 28.8 us  [send_back(): lax.psum_scatter(partial_value.astype(jnp.bfloat16), 'dev', scatter_dimen...]
    dot_general x1, matrix products: 3.05 us -> 0.72 us  [project_in(): jnp.einsum('epf,fh->eph', portion, gate_mat, preferred_element_type=jnp.f...]
  transfers between devices with their start and end apart: 6 -> 18, of which waited for: 4 -> 7; matrix products, arithmetic and copies ran while one was open for 15% -> 12% of each run, Pallas kernels for 0% -> 0%
where the time goes in v1:
time: 140 us; the launch traced here: 139 us
  waiting for transfers between devices  54.7 us (39%)
  blocking collectives  28.7 us (20%)
  starting transfers between devices  18.8 us (13%)
  matrix products  18.4 us (13%)
  between operations  14.4 us (10%)
  local copies, waits for them, and re-layouts  2.76 us (2%)
    reduce_scatter x2, waiting for transfers between devices, send_back(): lax.psum_scatter(partial_value.astype(jnp.bfloat16), 'dev', scatter_dimen...  28.8 us
    all_gather x2, blocking collectives, deliver(): whole_rows = lax.all_gather(local_rows, 'dev', axis=1, tiled=True)  28.7 us
    ppermute x14, waiting for transfers between devices, deliver(): part = lax.ppermute(part, 'node', [(d, d ^ mask) for d in range(ways)])  20.1 us
    ppermute x14, starting transfers between devices, deliver(): part = lax.ppermute(part, 'node', [(d, d ^ mask) for d in range(ways)])  11.4 us
    all_to_all x2, starting transfers between devices, send_back(): lax.all_to_all(shares, 'node', split_axis=0, concat_axis=0, tiled=True)  7.32 us
    all_to_all x2, waiting for transfers between devices, send_back(): lax.all_to_all(shares, 'node', split_axis=0, concat_axis=0, tiled=True)  5.79 us
    dot_general x1, matrix products, project_cotangent(): jnp.einsum('epf,hf->eph', portion, down_mat, preferred_element_type=jnp.f...  3.89 us
    dot_general x1, matrix products, project_cotangent(): jnp.einsum('eph,epf->hf', hidden, portion, preferred_element_type=jnp.flo...  3.29 us
  transfers between devices with their start and end apart: 18, of which 7 were waited for; matrix products, arithmetic and copies ran while one was open for 12% of the time, Pallas kernels for 0%

profile of v1, /device:TPU:0, one launch (start us, length us, event | category | flops | bytes accessed | tf_op | source)
XLA Modules:
  0.0 139.1 jit_solution(3084562002581130908)
XLA Ops:
  7.3 0.7 convert_multiply_fusion
  8.0 0.7 select_reduce_fusion
  8.8 15.3 %all_gather.6 = bf16[16,4096]{1,0:T(8,128)(2,1)S(1)} all-gather(bf16[16,1024]{1,0:T(8,128)(2,1)} %param.7), channel_id=1, replica_groups=mesh['node'=8,'dev'=4] {'dev'}, dimensions={1}, use_global_device_ids=true | all-gather | bytes 163840 | tf_op jit(solution)/shard_map/all_gather | solution.py:30
  24.9 2.5 %collective-permute-start.5 = (bf16[1,16,4096]{2,1,0:T(8,128)(2,1)S(1)}, bf16[1,16,4096]{2,1,0:T(8,128)(2,1)S(1)}, u32[]{:S(2)}, u32[]{:S(2)}) collective-permute-start(bf16[1,16,4096]{2,1,0:T(8,128)(2,1)S(1)} %get-tuple-element.14), channel_id=1, source_target_pairs={{0,24},{4,28},{8,16},{12,20},{16,8},{20,12},{24,0},{28,4},{1,25},{... | collective-permute-start | bytes 393224 | tf_op jit(solution)/shard_map/ppermute | solution.py:42
  27.4 1.4 collective-permute-start.4
  29.3 13.4 %all_gather.7 = bf16[16,4096]{1,0:T(8,128)(2,1)S(1)} all-gather(bf16[16,1024]{1,0:T(8,128)(2,1)S(1)} %copy-done.5), channel_id=1, replica_groups=mesh['node'=8,'dev'=4] {'dev'}, dimensions={1}, use_global_device_ids=true | all-gather | bytes 163840 | tf_op jit(solution)/shard_map/all_gather | solution.py:30
  42.7 1.1 convolution_convert_fusion
  44.0 1.5 %collective-permute-start.1 = (bf16[1,16,4096]{2,1,0:T(8,128)(2,1)S(1)}, bf16[1,16,4096]{2,1,0:T(8,128)(2,1)S(1)}, u32[]{:S(2)}, u32[]{:S(2)}) collective-permute-start(bf16[1,16,4096]{2,1,0:T(8,128)(2,1)S(1)} %get-tuple-element.18), channel_id=1, source_target_pairs={{0,8},{4,12},{8,0},{12,4},{16,24},{20,28},{24,16},{28,20},{1,9},{5... | collective-permute-start | bytes 393224 | tf_op jit(solution)/shard_map/ppermute | solution.py:42
  45.5 3.5 %collective-permute-done.1 = bf16[1,16,4096]{2,1,0:T(8,128)(2,1)S(1)} collective-permute-done((bf16[1,16,4096]{2,1,0:T(8,128)(2,1)S(1)}, bf16[1,16,4096]{2,1,0:T(8,128)(2,1)S(1)}, u32[]{:S(2)}, u32[]{:S(2)}) %collective-permute-start.1) | collective-permute-done | bytes 131104 | tf_op jit(solution)/shard_map/ppermute | solution.py:42
  49.0 5.7 %collective-permute-done.2 = bf16[1,16,4096]{2,1,0:T(8,128)(2,1)S(1)} collective-permute-done((bf16[1,16,4096]{2,1,0:T(8,128)(2,1)S(1)}, bf16[1,16,4096]{2,1,0:T(8,128)(2,1)S(1)}, u32[]{:S(2)}, u32[]{:S(2)}) %collective-permute-start.2) | collective-permute-done | bytes 131104 | tf_op jit(solution)/shard_map/ppermute | solution.py:42
  55.2 2.3 %collective-permute-start.12 = (bf16[1,16,4096]{2,1,0:T(8,128)(2,1)S(1)}, bf16[1,16,4096]{2,1,0:T(8,128)(2,1)S(1)}, u32[]{:S(2)}, u32[]{:S(2)}) collective-permute-start(bf16[1,16,4096]{2,1,0:T(8,128)(2,1)S(1)} %get-tuple-element.6), channel_id=1, source_target_pairs={{0,24},{4,28},{8,16},{12,20},{16,8},{20,12},{24,0},{28,4},{1,25},{... | collective-permute-start | bytes 393224 | tf_op jit(solution)/shard_map/ppermute | solution.py:42
  57.5 1.3 collective-permute-start.11
  58.9 0.6 collective-permute-start.10
  59.7 0.7 fusion.10
  60.4 0.7 multiply_convert_fusion.2
  61.2 1.4 %copy-done = bf16[1,512,4096]{2,1,0:T(8,128)(2,1)S(1)} copy-done((bf16[1,512,4096]{2,1,0:T(8,128)(2,1)S(1)}, bf16[1,512,4096]{2,1,0:T(8,128)(2,1)}, u32[]{:S(2)}) %copy-start) | copy-done | bytes 4194328
  62.6 1.7 %convolution_convert_fusion.1 = bf16[8,16,4096]{2,1,0:T(8,128)(2,1)} fusion(bf16[8,16,512]{2,1,0:T(8,128)(2,1)S(1)} %get-tuple-element.21, bf16[1,512,4096]{2,1,0:T(8,128)(2,1)S(1)} %copy-done), kind=kOutput, calls=%fused_computation.5 | convolution fusion | flops 537395200 | bytes 5373952 | tf_op jit(solution)/shard_map/eph,hf->epf/dot_general | solution.py:87
  64.4 0.6 collective-permute-start.8
  65.1 5.3 %collective-permute-done.8 = bf16[1,16,4096]{2,1,0:T(8,128)(2,1)S(1)} collective-permute-done((bf16[1,16,4096]{2,1,0:T(8,128)(2,1)S(1)}, bf16[1,16,4096]{2,1,0:T(8,128)(2,1)S(1)}, u32[]{:S(2)}, u32[]{:S(2)}) %collective-permute-start.8) | collective-permute-done | bytes 131104 | tf_op jit(solution)/shard_map/ppermute | solution.py:42
  70.4 5.6 %collective-permute-done.9 = bf16[1,16,4096]{2,1,0:T(8,128)(2,1)S(1)} collective-permute-done((bf16[1,16,4096]{2,1,0:T(8,128)(2,1)S(1)}, bf16[1,16,4096]{2,1,0:T(8,128)(2,1)S(1)}, u32[]{:S(2)}, u32[]{:S(2)}) %collective-permute-start.9) | collective-permute-done | bytes 131104 | tf_op jit(solution)/shard_map/ppermute | solution.py:42
  76.1 3.9 %fusion.2 = f32[8,16,512]{2,1,0:T(8,128)S(1)} fusion(bf16[8,16,4096]{2,1,0:T(8,128)(2,1)S(1)} %constant_dynamic-update-slice_fusion.6, bf16[1,512,4096]{2,1,0:T(8,128)(2,1)} %param.12), kind=kOutput, calls=%fused_computation.7 | convolution fusion | flops 536870912 | bytes 5505024 | tf_op jit(solution)/shard_map/epf,hf->eph/dot_general | solution.py:94
  80.0 1.5 %fusion.8 = f32[8,16,4096]{2,1,0:T(8,128)S(1)} fusion(bf16[1,4096,512]{2,1,0:T(8,128)(2,1)S(1)} %copy-done.2, f32[8,16,512]{2,1,0:T(8,128)S(1)} %fusion.10, f32[8,16,512]{2,1,0:T(8,128)S(1)} %fusion.2, f32[8,16,512]{2,1,0:T(8,128)S(1)} %get-tuple-element.22), kind=kOutput, calls=%fused_computation.13 | convolution fusion | flops 537526272 | bytes 7077888 | tf_op jit(solution)/shard_map/eph,fh->epf/dot_general | solution.py:106
  81.5 0.7 copy-done.4
  82.2 2.5 %fusion.1 = bf16[8,16,4096]{2,1,0:T(8,128)(2,1)} fusion(f32[8,16,4096]{2,1,0:T(8,128)S(1)} %fusion.8, bf16[1,4096,512]{2,1,0:T(8,128)(2,1)S(1)} %copy-done.4, f32[8,16,512]{2,1,0:T(8,128)S(1)} %fusion.2, f32[8,16,512]{2,1,0:T(8,128)S(1)} %fusion.10), kind=kOutput, calls=%fused_computation.3 | convolution fusion | flops 538312704 | bytes 7864320 | tf_op jit(solution)/shard_map/eph,fh->epf/dot_general | solution.py:109
  84.8 7.5 %reduce-scatter.3.cloned.1.call-done = bf16[8,16,1024]{2,1,0:T(8,128)(2,1)} async-done(((bf16[8,16,4096]{2,1,0:T(8,128)(2,1)}), bf16[8,16,1024]{2,1,0:T(8,128)(2,1)}) %reduce-scatter.3.cloned.1.call-update) | async-done | bytes 262160 | tf_op jit(solution)/shard_map/reduce_scatter | solution.py:49
  92.3 3.7 %all-to-all-start = ((bf16[8,16,1024]{2,1,0:T(8,128)(2,1)}), bf16[8,16,1024]{2,1,0:T(8,128)(2,1)S(1)}, u32[]{:S(2)}, u32[]{:S(2)}) async-start(bf16[8,16,1024]{2,1,0:T(8,128)(2,1)} %reduce-scatter.3.cloned.1.call-done), calls=%async_computation.1 | async-start | bytes 524288 | tf_op jit(solution)/shard_map/all_to_all | solution.py:52
  96.0 3.3 %fusion = bf16[1,512,4096]{2,1,0:T(8,128)(2,1)} fusion(bf16[8,16,512]{2,1,0:T(8,128)(2,1)S(1)} %get-tuple-element.21, bf16[8,16,4096]{2,1,0:T(8,128)(2,1)S(1)} %constant_dynamic-update-slice_fusion.6), kind=kOutput, calls=%fused_computation.1 | convolution fusion | flops 538968064 | bytes 5373952 | tf_op jit(solution)/shard_map/eph,epf->hf/dot_general | solution.py:95
  99.2 21.3 %reduce-scatter.5.cloned.1.call-done = bf16[8,16,1024]{2,1,0:T(8,128)(2,1)} async-done(((bf16[8,16,4096]{2,1,0:T(8,128)(2,1)}), bf16[8,16,1024]{2,1,0:T(8,128)(2,1)}) %reduce-scatter.5.cloned.1.call-update) | async-done | bytes 262160 | tf_op jit(solution)/shard_map/reduce_scatter | solution.py:49
  120.5 3.6 %all-to-all-start.1 = ((bf16[8,16,1024]{2,1,0:T(8,128)(2,1)}), bf16[8,16,1024]{2,1,0:T(8,128)(2,1)S(1)}, u32[]{:S(2)}, u32[]{:S(2)}) async-start(bf16[8,16,1024]{2,1,0:T(8,128)(2,1)} %reduce-scatter.5.cloned.1.call-done), calls=%async_computation.3 | async-start | bytes 524288 | tf_op jit(solution)/shard_map/all_to_all | solution.py:52
  124.1 1.1 fusion.12
  125.3 5.8 %all-to-all-done.1 = bf16[8,16,1024]{2,1,0:T(8,128)(2,1)S(1)} async-done(((bf16[8,16,1024]{2,1,0:T(8,128)(2,1)}), bf16[8,16,1024]{2,1,0:T(8,128)(2,1)S(1)}, u32[]{:S(2)}, u32[]{:S(2)}) %all-to-all-start.1) | async-done | bytes 262176 | tf_op jit(solution)/shard_map/all_to_all | solution.py:52
  131.1 1.1 fusion.13
  (53 shorter events, 2.5 us)
Async XLA Ops:
  7.2 22.1 %copy-start.5 = (bf16[16,1024]{1,0:T(8,128)(2,1)S(1)}, bf16[16,1024]{1,0:T(8,128)(2,1)}, u32[]{:S(2)}) copy-start(bf16[16,1024]{1,0:T(8,128)(2,1)} %param.13) | copy-start | bytes 98308
  7.2 85.1 %reduce-scatter.3.cloned.1.call-start = ((), (), s32[]{:S(2)}) async-start(), calls=%async_computation.4 | async-start | bytes 1310720 | tf_op jit(solution)/shard_map/reduce_scatter | solution.py:49
  24.7 35.0 %copy-start.1 = (bf16[1,4096,512]{2,1,0:T(8,128)(2,1)S(1)}, bf16[1,4096,512]{2,1,0:T(8,128)(2,1)}, u32[]{:S(2)}) copy-start(bf16[1,4096,512]{2,1,0:T(8,128)(2,1)} %param.10) | copy-start | bytes 12582916
  24.8 34.7 %collective-permute-start.6 = (bf16[1,16,4096]{2,1,0:T(8,128)(2,1)S(1)}, bf16[1,16,4096]{2,1,0:T(8,128)(2,1)S(1)}, u32[]{:S(2)}, u32[]{:S(2)}) collective-permute-start(bf16[1,16,4096]{2,1,0:T(8,128)(2,1)S(1)} %get-tuple-element.13), channel_id=1, source_target_pairs={{0,28},{4,24},{8,20},{12,16},{16,12},{20,8},{24,4},{28,0},{1,29},{... | collective-permute-start | bytes 393224 | tf_op jit(solution)/shard_map/ppermute | solution.py:42
  24.9 34.0 %collective-permute-start.5 = (bf16[1,16,4096]{2,1,0:T(8,128)(2,1)S(1)}, bf16[1,16,4096]{2,1,0:T(8,128)(2,1)S(1)}, u32[]{:S(2)}, u32[]{:S(2)}) collective-permute-start(bf16[1,16,4096]{2,1,0:T(8,128)(2,1)S(1)} %get-tuple-element.14), channel_id=1, source_target_pairs={{0,24},{4,28},{8,16},{12,20},{16,8},{20,12},{24,0},{28,4},{1,25},{... | collective-permute-start | bytes 393224 | tf_op jit(solution)/shard_map/ppermute | solution.py:42
  27.4 30.1 %collective-permute-start.4 = (bf16[1,16,4096]{2,1,0:T(8,128)(2,1)S(1)}, bf16[1,16,4096]{2,1,0:T(8,128)(2,1)S(1)}, u32[]{:S(2)}, u32[]{:S(2)}) collective-permute-start(bf16[1,16,4096]{2,1,0:T(8,128)(2,1)S(1)} %get-tuple-element.15), channel_id=1, source_target_pairs={{0,20},{4,16},{8,28},{12,24},{16,4},{20,0},{24,12},{28,8},{1,21},{... | collective-permute-start | bytes 393224 | tf_op jit(solution)/shard_map/ppermute | solution.py:42
  28.8 26.4 %collective-permute-start.3 = (bf16[1,16,4096]{2,1,0:T(8,128)(2,1)S(1)}, bf16[1,16,4096]{2,1,0:T(8,128)(2,1)S(1)}, u32[]{:S(2)}, u32[]{:S(2)}) collective-permute-start(bf16[1,16,4096]{2,1,0:T(8,128)(2,1)S(1)} %get-tuple-element.16), channel_id=1, source_target_pairs={{0,16},{4,20},{8,24},{12,28},{16,0},{20,4},{24,8},{28,12},{1,17},{... | collective-permute-start | bytes 393224 | tf_op jit(solution)/shard_map/ppermute | solution.py:42
  29.3 14.7 %collective-permute-start = (bf16[1,16,4096]{2,1,0:T(8,128)(2,1)S(1)}, bf16[1,16,4096]{2,1,0:T(8,128)(2,1)S(1)}, u32[]{:S(2)}, u32[]{:S(2)}) collective-permute-start(bf16[1,16,4096]{2,1,0:T(8,128)(2,1)S(1)} %get-tuple-element.19), channel_id=1, source_target_pairs={{0,4},{4,0},{8,12},{12,8},{16,20},{20,16},{24,28},{28,24},{1,5},{5... | collective-permute-start | bytes 393224 | tf_op jit(solution)/shard_map/ppermute | solution.py:42
  44.0 5.0 %collective-permute-start.1 = (bf16[1,16,4096]{2,1,0:T(8,128)(2,1)S(1)}, bf16[1,16,4096]{2,1,0:T(8,128)(2,1)S(1)}, u32[]{:S(2)}, u32[]{:S(2)}) collective-permute-start(bf16[1,16,4096]{2,1,0:T(8,128)(2,1)S(1)} %get-tuple-element.18), channel_id=1, source_target_pairs={{0,8},{4,12},{8,0},{12,4},{16,24},{20,28},{24,16},{28,20},{1,9},{5... | collective-permute-start | bytes 393224 | tf_op jit(solution)/shard_map/ppermute | solution.py:42
  49.0 11.4 %copy-start.3 = (bf16[1,4096,512]{2,1,0:T(8,128)(2,1)S(1)}, bf16[1,4096,512]{2,1,0:T(8,128)(2,1)}, u32[]{:S(2)}) copy-start(bf16[1,4096,512]{2,1,0:T(8,128)(2,1)} %param.11) | copy-start | bytes 12582916
  49.0 5.8 %collective-permute-start.2 = (bf16[1,16,4096]{2,1,0:T(8,128)(2,1)S(1)}, bf16[1,16,4096]{2,1,0:T(8,128)(2,1)S(1)}, u32[]{:S(2)}, u32[]{:S(2)}) collective-permute-start(bf16[1,16,4096]{2,1,0:T(8,128)(2,1)S(1)} %get-tuple-element.17), channel_id=1, source_target_pairs={{0,12},{4,8},{8,4},{12,0},{16,28},{20,24},{24,20},{28,16},{1,13},{... | collective-permute-start | bytes 393224 | tf_op jit(solution)/shard_map/ppermute | solution.py:42
  54.8 21.3 %collective-permute-start.13 = (bf16[1,16,4096]{2,1,0:T(8,128)(2,1)S(1)}, bf16[1,16,4096]{2,1,0:T(8,128)(2,1)S(1)}, u32[]{:S(2)}, u32[]{:S(2)}) collective-permute-start(bf16[1,16,4096]{2,1,0:T(8,128)(2,1)S(1)} %get-tuple-element.5), channel_id=1, source_target_pairs={{0,28},{4,24},{8,20},{12,16},{16,12},{20,8},{24,4},{28,0},{1,29},{... | collective-permute-start | bytes 393224 | tf_op jit(solution)/shard_map/ppermute | solution.py:42
  55.2 20.9 %collective-permute-start.12 = (bf16[1,16,4096]{2,1,0:T(8,128)(2,1)S(1)}, bf16[1,16,4096]{2,1,0:T(8,128)(2,1)S(1)}, u32[]{:S(2)}, u32[]{:S(2)}) collective-permute-start(bf16[1,16,4096]{2,1,0:T(8,128)(2,1)S(1)} %get-tuple-element.6), channel_id=1, source_target_pairs={{0,24},{4,28},{8,16},{12,20},{16,8},{20,12},{24,0},{28,4},{1,25},{... | collective-permute-start | bytes 393224 | tf_op jit(solution)/shard_map/ppermute | solution.py:42
  57.5 18.5 %collective-permute-start.11 = (bf16[1,16,4096]{2,1,0:T(8,128)(2,1)S(1)}, bf16[1,16,4096]{2,1,0:T(8,128)(2,1)S(1)}, u32[]{:S(2)}, u32[]{:S(2)}) collective-permute-start(bf16[1,16,4096]{2,1,0:T(8,128)(2,1)S(1)} %get-tuple-element.7), channel_id=1, source_target_pairs={{0,20},{4,16},{8,28},{12,24},{16,4},{20,0},{24,12},{28,8},{1,21},{... | collective-permute-start | bytes 393224 | tf_op jit(solution)/shard_map/ppermute | solution.py:42
  58.9 17.1 %collective-permute-start.10 = (bf16[1,16,4096]{2,1,0:T(8,128)(2,1)S(1)}, bf16[1,16,4096]{2,1,0:T(8,128)(2,1)S(1)}, u32[]{:S(2)}, u32[]{:S(2)}) collective-permute-start(bf16[1,16,4096]{2,1,0:T(8,128)(2,1)S(1)} %get-tuple-element.8), channel_id=1, source_target_pairs={{0,16},{4,20},{8,24},{12,28},{16,0},{20,4},{24,8},{28,12},{1,17},{... | collective-permute-start | bytes 393224 | tf_op jit(solution)/shard_map/ppermute | solution.py:42
  59.5 4.9 %collective-permute-start.7 = (bf16[1,16,4096]{2,1,0:T(8,128)(2,1)S(1)}, bf16[1,16,4096]{2,1,0:T(8,128)(2,1)S(1)}, u32[]{:S(2)}, u32[]{:S(2)}) collective-permute-start(bf16[1,16,4096]{2,1,0:T(8,128)(2,1)S(1)} %get-tuple-element.11), channel_id=1, source_target_pairs={{0,4},{4,0},{8,12},{12,8},{16,20},{20,16},{24,28},{28,24},{1,5},{5... | collective-permute-start | bytes 393224 | tf_op jit(solution)/shard_map/ppermute | solution.py:42
  60.4 2.2 %copy-start = (bf16[1,512,4096]{2,1,0:T(8,128)(2,1)S(1)}, bf16[1,512,4096]{2,1,0:T(8,128)(2,1)}, u32[]{:S(2)}) copy-start(bf16[1,512,4096]{2,1,0:T(8,128)(2,1)} %param.12) | copy-start | bytes 12582916
  64.4 56.1 %reduce-scatter.5.cloned.1.call-start = ((), (), s32[]{:S(2)}) async-start(), calls=%async_computation.5 | async-start | bytes 1310720 | tf_op jit(solution)/shard_map/reduce_scatter | solution.py:49
  64.4 5.9 %collective-permute-start.8 = (bf16[1,16,4096]{2,1,0:T(8,128)(2,1)S(1)}, bf16[1,16,4096]{2,1,0:T(8,128)(2,1)S(1)}, u32[]{:S(2)}, u32[]{:S(2)}) collective-permute-start(bf16[1,16,4096]{2,1,0:T(8,128)(2,1)S(1)} %get-tuple-element.10), channel_id=1, source_target_pairs={{0,8},{4,12},{8,0},{12,4},{16,24},{20,28},{24,16},{28,20},{1,9},{5... | collective-permute-start | bytes 393224 | tf_op jit(solution)/shard_map/ppermute | solution.py:42
  70.3 5.6 %collective-permute-start.9 = (bf16[1,16,4096]{2,1,0:T(8,128)(2,1)S(1)}, bf16[1,16,4096]{2,1,0:T(8,128)(2,1)S(1)}, u32[]{:S(2)}, u32[]{:S(2)}) collective-permute-start(bf16[1,16,4096]{2,1,0:T(8,128)(2,1)S(1)} %get-tuple-element.9), channel_id=1, source_target_pairs={{0,12},{4,8},{8,4},{12,0},{16,28},{20,24},{24,20},{28,16},{1,13},{... | collective-permute-start | bytes 393224 | tf_op jit(solution)/shard_map/ppermute | solution.py:42
  76.1 3.9 %copy-start.2 = (bf16[1,4096,512]{2,1,0:T(8,128)(2,1)S(1)}, bf16[1,4096,512]{2,1,0:T(8,128)(2,1)}, u32[]{:S(2)}) copy-start(bf16[1,4096,512]{2,1,0:T(8,128)(2,1)} %param.10) | copy-start | bytes 12582916
  80.0 2.2 %copy-start.4 = (bf16[1,4096,512]{2,1,0:T(8,128)(2,1)S(1)}, bf16[1,4096,512]{2,1,0:T(8,128)(2,1)}, u32[]{:S(2)}) copy-start(bf16[1,4096,512]{2,1,0:T(8,128)(2,1)} %param.11) | copy-start | bytes 12582916
  92.3 28.2 %all-to-all-start = ((bf16[8,16,1024]{2,1,0:T(8,128)(2,1)}), bf16[8,16,1024]{2,1,0:T(8,128)(2,1)S(1)}, u32[]{:S(2)}, u32[]{:S(2)}) async-start(bf16[8,16,1024]{2,1,0:T(8,128)(2,1)} %reduce-scatter.3.cloned.1.call-done), calls=%async_computation.1 | async-start | bytes 524288 | tf_op jit(solution)/shard_map/all_to_all | solution.py:52
  120.5 10.6 %all-to-all-start.1 = ((bf16[8,16,1024]{2,1,0:T(8,128)(2,1)}), bf16[8,16,1024]{2,1,0:T(8,128)(2,1)S(1)}, u32[]{:S(2)}, u32[]{:S(2)}) async-start(bf16[8,16,1024]{2,1,0:T(8,128)(2,1)} %reduce-scatter.5.cloned.1.call-done), calls=%async_computation.3 | async-start | bytes 524288 | tf_op jit(solution)/shard_map/all_to_all | solution.py:52
Sparse Core Ops, SparseCore 0:
  64.5 27.7 reduce-scatter.2
  94.7 25.7 reduce-scatter.4
